TPU v7x, 32 devices: a whole 2x2x4 slice. The times are simulated.
32 devices in a mesh: row: 8 (over y, x, core), col: 4 (over z).
Axes of the slice: x: 2, y: 2, z: 4, core: 2. Of those that a mesh axis runs over, the one named last changes fastest.
Arguments:
- source_v: float32 [2, 4, 2560, 768], P(None, 'col', 'row'), may hold values from -6 to 6
- source_omega: float32 [2, 4, 2560, 768], P(None, 'col', 'row'), may hold values from -6 to 6
- forward_map: float32 [768, 768], P('col'), may hold values from -0.21875 to 0.21875
- back_maps: float32 [2, 768, 768], P(None, 'col'), may hold values from -0.21875 to 0.21875
- eigenvalues: float32 [768], replicated, may hold values from 0.02 to 4
- penalty: float32 [768, 3840], P('row'), may hold values from 0.05 to 4
Outputs:
- v_field: float32 [2, 4, 2560, 768], P(None, 'col', 'row')
- omega_field: float32 [2, 4, 2560, 768], P(None, 'col', 'row')
All inputs are finite; a program needn't handle non-finite values.
Results may differ from a plain program's by a relative error of at most 0.000098.
Values sent between devices are 32-bit elements; how exact they have to be, the bound alone decides.
A program may use at most 128 MiB of HBM per device.

v0:
```python
import math
import jax
import jax.numpy as jnp
from jax import lax
from jax.sharding import PartitionSpec as P


def helm_scale(eigen_part, flow_wave, span_wave):
    return 1.0 / (1.0 + eigen_part + 0.05 * (flow_wave * flow_wave + span_wave * span_wave))


def form_velocity(flow_wave, span_wave, derivative, vorticity):
    wave_sq = jnp.maximum(flow_wave * flow_wave + span_wave * span_wave, 1.0)
    along_real = (span_wave * vorticity[1] - flow_wave * derivative[1]) / wave_sq
    along_imag = (flow_wave * derivative[0] - span_wave * vorticity[0]) / wave_sq
    across_real = -(span_wave * derivative[1] + flow_wave * vorticity[1]) / wave_sq
    across_imag = (span_wave * derivative[0] + flow_wave * vorticity[0]) / wave_sq
    return (jnp.stack([along_real, along_imag]), jnp.stack([across_real, across_imag]))


def form_vorticity(flow_wave, span_wave, along, across):
    real_part = flow_wave * across[1] - span_wave * along[1]
    imag_part = span_wave * along[0] - flow_wave * across[0]
    return jnp.stack([real_part, imag_part])


def spanwise_tables(blocks_k, blocks_z, count_z):
    coarse_k = jnp.arange(blocks_k, dtype=jnp.int32)
    coarse_k = jnp.where(coarse_k < blocks_k // 2, coarse_k, coarse_k + blocks_z - blocks_k)
    coarse_z = jnp.arange(blocks_z, dtype=jnp.int32)
    fine_index = jnp.arange(128, dtype=jnp.int32)
    coarse_angle = (
        2.0
        * math.pi
        / blocks_z
        * (coarse_z[:, None] * coarse_k[None, :] % blocks_z).astype(jnp.float32)
    )
    twist_angle = (
        2.0
        * math.pi
        / count_z
        * (coarse_z[:, None] * fine_index[None, :] % count_z).astype(jnp.float32)
    )
    fine_angle = (
        2.0 * math.pi / 128 * (fine_index[:, None] * fine_index[None, :] % 128).astype(jnp.float32)
    )
    return (coarse_angle, twist_angle, fine_angle)


def block_table(cos_part, sin_part, axis_in):
    first = jnp.stack([cos_part, -sin_part], axis=axis_in)
    second = jnp.stack([sin_part, cos_part], axis=axis_in)
    return jnp.stack([first, second], axis=0)


def twist_apply(data, twist_cos, twist_sin):
    real_part = data[:, 0]
    imag_part = data[:, 1]
    return jnp.stack(
        [
            real_part * twist_cos - imag_part * twist_sin,
            real_part * twist_sin + imag_part * twist_cos,
        ],
        axis=1,
    )


def spanwise_pass(spanwise, factor_grid, count_z):
    count_kz = spanwise.shape[-1]
    blocks_k = count_kz // 128
    blocks_z = count_z // 128
    lead = spanwise.shape[:4]
    data = spanwise.reshape(lead + (blocks_k, 128))
    coarse_angle, twist_angle, fine_angle = spanwise_tables(blocks_k, blocks_z, count_z)
    coarse_cos, coarse_sin = (jnp.cos(coarse_angle), jnp.sin(coarse_angle))
    twist_cos, twist_sin = (jnp.cos(twist_angle), jnp.sin(twist_angle))
    fine_cos, fine_sin = (jnp.cos(fine_angle), jnp.sin(fine_angle))
    coarse_fwd = block_table(coarse_cos, coarse_sin, 1)
    fine_fwd = block_table(fine_cos, fine_sin, 1)
    fine_inv = block_table(fine_cos, -fine_sin, 1)
    coarse_inv = jnp.transpose(block_table(coarse_cos, -coarse_sin, 1), (0, 2, 1, 3)) / count_z
    data = jnp.einsum("cadk,fdxyks->fcxyas", coarse_fwd, data, precision=lax.Precision.HIGHEST)
    data = twist_apply(data, twist_cos, twist_sin)
    data = jnp.einsum("cnds,fdxyas->fcxyan", fine_fwd, data, precision=lax.Precision.HIGHEST)
    data = data * factor_grid
    data = jnp.einsum("ckdn,fdxyan->fcxyak", fine_inv, data, precision=lax.Precision.HIGHEST)
    data = twist_apply(data, twist_cos, -twist_sin)
    data = jnp.einsum("cdak,fdxyas->fcxyks", coarse_inv, data, precision=lax.Precision.HIGHEST)
    return data.reshape(lead + (count_kz,))


def shards(source_v, source_omega, forward_map, back_maps, eigenvalues, penalty):
    local_kx = source_v.shape[1]
    local_kz = source_v.shape[2]
    count_kz = local_kz * lax.axis_size("row")
    half_kz = count_kz // 2
    local_y = penalty.shape[0]
    count_z = penalty.shape[1]
    flow_index = lax.axis_index("col") * local_kx + jnp.arange(local_kx, dtype=jnp.int32)
    flow_wave = 0.5 * flow_index.astype(jnp.float32)
    span_index = lax.axis_index("row") * local_kz + jnp.arange(local_kz, dtype=jnp.int32)
    span_local = (
        jnp.where(span_index < half_kz, span_index, span_index - count_kz).astype(jnp.float32)
        * 8.0
        / half_kz
    )
    scaling = helm_scale(
        eigenvalues[None, None, :], flow_wave[:, None, None], span_local[None, :, None]
    )
    sources = jnp.stack([source_v, source_omega])
    flow_column = flow_wave[:, None, None]
    span_row = span_local[None, None, :]
    partial_coeffs = jnp.einsum(
        "fcxkn,jn->fcxkj",
        sources,
        lax.all_gather(forward_map, "col", axis=0, tiled=True),
        precision=lax.Precision.HIGHEST,
    )
    coeffs = partial_coeffs * scaling
    block_rows = lax.all_gather(back_maps, "col", axis=1, tiled=True)
    values = jnp.einsum("yj,fcxkj->fcxyk", block_rows[0], coeffs, precision=lax.Precision.HIGHEST)
    derivative = jnp.einsum(
        "yj,cxkj->cxyk", block_rows[1], coeffs[0], precision=lax.Precision.HIGHEST
    )
    along, across = form_velocity(flow_column, span_row, derivative, values[1])
    fields = jnp.stack([along, values[0], across])
    spanwise = lax.all_to_all(fields, "row", split_axis=3, concat_axis=4, tiled=True)
    factor_grid = jnp.transpose(
        (1.0 / (1.0 + penalty)).reshape(local_y, 128, count_z // 128), (0, 2, 1)
    )
    result = spanwise_pass(spanwise, factor_grid, count_z)
    returned = lax.all_to_all(result, "row", split_axis=4, concat_axis=3, tiled=True)
    v_part = returned[1]
    omega_part = form_vorticity(flow_column, span_row, returned[0], returned[2])
    return (jnp.transpose(v_part, (0, 1, 3, 2)), jnp.transpose(omega_part, (0, 1, 3, 2)))


def solution(mesh):
    placed = (
        P(None, "col", "row", None),
        P(None, "col", "row", None),
        P("col", None),
        P(None, "col", None),
        P(),
        P("row", None),
    )
    return jax.shard_map(
        shards,
        mesh=mesh,
        in_specs=placed,
        out_specs=(P(None, "col", "row", None), P(None, "col", "row", None)),
        check_vma=False,
    )
```

profile of v0, /device:TPU:0, one launch (start us, length us, event | category | flops | bytes accessed | tf_op | source)
XLA Modules:
  0.0 500.1 jit_solution(2554494599906409312)
XLA Ops:
  7.2 0.0 all-gather.3.cloned.1.call-start
  7.2 0.7 all-gather.3.cloned.1.call-update
  7.9 0.0 all-gather.5.cloned.1.call-start
  7.9 0.7 all-gather.5.cloned.1.call-update
  8.7 0.7 broadcast_add_fusion
  9.4 0.2 add_divide_fusion.2
  9.6 53.2 %all-gather.3.cloned.1.call-done = f32[768,768]{1,0:T(8,128)} async-done(((f32[192,768]{1,0:T(8,128)}), f32[768,768]{1,0:T(8,128)}) %all-gather.3.cloned.1.call-update) | async-done | bytes 2359312 | tf_op jit(solution)/shard_map/all_gather | solution.py:116
  62.8 13.7 %fusion.23 = f32[2,2,320,768]{3,2,1,0:T(8,128)} fusion(f32[768,768]{1,0:T(8,128)} %all-gather.3.cloned.1.call-done, f32[1,2,1,320,768]{4,3,1,0,2:T(8,128)} %bitcast.194, f32[1,2,1,320,768]{4,3,1,0,2:T(8,128)} %bitcast.195, f32[320,768]{1,0:T(8,128)S(1)} %add_divide_fusion.2), kind=kOutput, calls=%fused_computation.31 | convolution fusion | flops 9061662720 | bytes 11206656 | tf_op jit(solution)/shard_map/fcxkn,jn->fcxkj/dot_general | solution.py:113
  76.5 76.1 %all-gather.5.cloned.1.call-done = f32[2,768,768]{2,1,0:T(8,128)} async-done(((f32[2,192,768]{2,1,0:T(8,128)}), f32[2,768,768]{2,1,0:T(8,128)}) %all-gather.5.cloned.1.call-update) | async-done | bytes 4718608 | tf_op jit(solution)/shard_map/all_gather | solution.py:120
  152.6 13.3 %fusion.21 = f32[2,2,320,768]{3,2,1,0:T(8,128)S(1)} fusion(f32[2,2,320,768]{3,2,1,0:T(8,128)} %fusion.23, f32[2,768,768]{2,1,0:T(8,128)} %all-gather.5.cloned.1.call-done), kind=kOutput, calls=%fused_computation.29 | convolution fusion | flops 9059696640 | bytes 10223616 | tf_op jit(solution)/shard_map/yj,fcxkj->fcxyk/dot_general | solution.py:121
  165.9 0.1 slice.98
  166.0 0.0 copy-done
  166.0 0.0 copy-done.2
  166.0 5.5 %fusion.26 = f32[2,1,768,320]{2,3,0,1:T(8,128)S(1)} fusion(f32[2,768,768]{2,1,0:T(8,128)S(1)} %copy-done.2, f32[2,2,320,768]{3,2,1,0:T(8,128)S(1)} %copy-done), kind=kOutput, calls=%fused_computation.36 | convolution fusion | flops 4529848320 | bytes 6291456 | tf_op jit(solution)/shard_map/yj,cxkj->cxyk/dot_general | solution.py:122
  171.5 0.7 subtract_divide_fusion.1
  172.2 0.1 maximum_bitcast_fusion.9
  172.4 0.1 maximum_bitcast_fusion.10
  172.5 2.9 pad_maximum_fusion
  175.5 13.2 %copy.41 = f32[3,2,1,768,320]{4,1,0,2,3:T(2,128)} copy(f32[3,2,1,768,320]{3,4,1,0,2:T(8,128)} %pad_maximum_fusion) | data formatting | bytes 11796480 | tf_op jit(solution)/shard_map/stack | solution.py:126
  188.7 5.0 all-to-all-start
  193.6 0.0 copy-done.6
  193.6 0.2 add_divide_fusion
  193.8 1.8 copy.46
  195.6 1.6 reshape.757
  197.2 1.8 copy.47
  199.0 0.7 fusion.69
  199.7 0.7 fusion.59
  200.4 0.3 fusion.49
  200.6 0.1 fusion.70
  200.8 0.6 fusion.53
  201.4 0.3 fusion.47
  201.7 71.9 %all-to-all-done = f32[3,2,1,768,320]{4,1,0,2,3:T(2,128)} async-done(((f32[3,2,1,768,320]{4,1,0,2,3:T(2,128)}), f32[3,2,1,768,320]{4,1,0,2,3:T(2,128)}, u32[]{:S(2)}, u32[]{:S(2)}) %all-to-all-start) | async-done | bytes 5898272 | tf_op jit(solution)/shard_map/all_to_all | solution.py:127
  273.7 3.5 copy.42
  277.1 7.0 %copy.77 = f32[3,2,1,96,8,320]{5,4,1,3,0,2:T(8,128)} copy(f32[3,2,1,96,8,320]{5,3,4,1,0,2:T(8,128)S(1)} %bitcast.185) | data formatting | bytes 11796480 | tf_op jit(solution)/shard_map/reshape.27
  284.1 9.5 %reshape.764 = f32[3,2,96,20,128,1]{4,3,1,2,0,5:T(8,128)} reshape(f32[3,2,1,96,8,320]{5,4,1,3,0,2:T(8,128)} %copy.77) | data formatting | bytes 11796480 | tf_op jit(solution)/shard_map/reshape.27
  293.6 10.7 %fusion.13 = f32[3,2,1,96,30,128]{5,4,1,3,0,2:T(8,128)S(1)} fusion(f32[3,2,96,20,128,1]{4,3,1,2,0,5:T(8,128)} %reshape.764, f32[1,30,2,20]{1,3,2,0:T(8,128)S(1)} %get-tuple-element.27, f32[1,30,2,20]{1,3,2,0:T(8,128)S(1)} %get-tuple-element.30), kind=kOutput, calls=%fused_computation.23 | convolution fusion | flops 1061685632 | bytes 14755200 | tf_op jit(solution)/shard_map/cadk,fdxyks->fcxyas/dot_general | solution.py:82
  304.3 2.5 multiply_subtract_fusion.1
  306.8 1.6 maximum_bitcast_fusion
  308.3 0.0 copy-start.1
  308.3 13.7 %fusion.5 = f32[3,96,30,2,128,1]{4,1,5,3,2,0:T(8,128)S(1)} fusion(f32[3,2,96,30,128,1]{4,3,1,2,0,5:T(8,128)S(1)} %maximum_bitcast_fusion, f32[1,128,2,128]{3,1,2,0:T(8,128)S(1)} %get-tuple-element.21, f32[1,128,2,128]{3,1,2,0:T(8,128)S(1)} %get-tuple-element.24), kind=kOutput, calls=%fused_computation.9 | convolution fusion | flops 6794838016 | bytes 17956864 | tf_op jit(solution)/shard_map/cnds,fdxyas->fcxyan/dot_general | solution.py:84
  322.1 0.0 copy-done.1
  322.1 7.6 %fusion.16 = f32[3,96,30,2,128]{4,1,3,2,0:T(8,128)S(1)} fusion(f32[3,96,30,2,128,1]{4,1,5,3,2,0:T(8,128)S(1)} %fusion.5, f32[96,30,128]{2,0,1:T(8,128)S(1)} %copy-done.1, f32[1,128,2,128]{3,1,2,0:T(8,128)S(1)} %get-tuple-element.25, f32[1,128,2,128]{3,1,2,0:T(8,128)S(1)} %get-tuple-element.20), kind=kOutput, calls=%fused_computation.24 | convolution fusion | flops 6797049856 | bytes 19431424 | tf_op jit(solution)/shard_map/ckdn,fdxyan->fcxyak/dot_general | solution.py:86
  329.7 5.4 %copy.88 = f32[3,96,30,2,128]{4,2,3,1,0:T(8,128)S(1)} copy(f32[3,96,30,2,128]{4,1,3,2,0:T(8,128)S(1)} %fusion.16) | data formatting | bytes 17694720 | tf_op jit(solution)/shard_map/ckdn,fdxyan->fcxyak/dot_general | solution.py:86
  335.0 0.0 copy-done.9
  335.0 0.0 copy-start.7
  335.1 1.8 multiply_subtract_fusion
  336.9 10.1 %fusion.19 = f32[3,2,1,96,20,128]{5,4,1,3,0,2:T(8,128)} fusion(f32[3,1,1,96,30,128]{5,4,1,3,0,2:T(8,128)S(1)} %get-tuple-element.9, f32[3,1,1,96,30,128]{5,4,1,3,0,2:T(8,128)S(1)} %get-tuple-element.8, f32[1,30,2,20]{1,3,2,0:T(8,128)S(1)} %copy-done.8, f32[1,30,2,20]{1,3,2,0:T(8,128)S(1)} %copy-done.7), kind=kOutput, calls=%fused_computation.25 | convolution fusion | flops 1063899840 | bytes 14755200 | tf_op jit(solution)/shard_map/cdak,fdxyas->fcxyks/dot_general | solution.py:88
  347.0 10.4 %copy.84 = f32[3,2,1,96,20,128]{3,1,0,5,4,2:T(2,128)} copy(f32[3,2,1,96,20,128]{5,4,1,3,0,2:T(8,128)} %fusion.19) | data formatting | bytes 11796480 | tf_op jit(solution)/shard_map/reshape | solution.py:89
  357.4 94.0 %all_to_all.30 = f32[3,2,1,96,2560]{3,1,0,2,4:T(2,128)} all-to-all(f32[3,2,1,96,2560]{3,1,0,2,4:T(2,128)} %bitcast.181), channel_id=1, replica_groups=mesh['row'=8,'col'=4] {'row'}, dimensions={4} | all-to-all | bytes 11796480 | tf_op jit(solution)/shard_map/all_to_all | solution.py:132
  451.4 9.9 %copy.82 = f32[3,2,1,96,8,320]{5,4,3,1,0,2:T(8,128)} copy(f32[3,2,1,96,8,320]{3,1,0,5,4,2:T(2,128)} %bitcast.182) | data formatting | bytes 11796480 | tf_op jit(solution)/shard_map/all_to_all | solution.py:132
  461.2 4.0 fusion.81
  465.3 1.8 slice.103
  467.1 1.3 copy.54
  468.4 2.6 copy.55
  470.9 2.5 copy.53
  473.5 2.6 copy.56
  476.1 2.5 copy.57
  478.6 2.6 copy.58
  481.2 1.2 copy.59
  482.4 2.6 copy.60
  485.0 1.9 copy.52
  486.9 3.1 copy.61
  490.0 1.5 multiply_subtract_fusion.3
  491.4 1.4 maximum_bitcast_fusion.11
  (17 shorter events, 0.1 us)
Async XLA Ops:
  7.2 55.6 %all-gather.3.cloned.1.call-start = ((), (), s32[]{:S(2)}) async-start(), calls=%async_computation.2 | async-start | bytes 2949120 | tf_op jit(solution)/shard_map/all_gather | solution.py:116
  7.9 144.7 %all-gather.5.cloned.1.call-start = ((), (), s32[]{:S(2)}) async-start(), calls=%async_computation.3 | async-start | bytes 5898240 | tf_op jit(solution)/shard_map/all_gather | solution.py:120
  152.6 13.4 %copy-start = (f32[2,2,320,768]{3,2,1,0:T(8,128)S(1)}, f32[2,2,320,768]{3,2,1,0:T(8,128)}, u32[]{:S(2)}) copy-start(f32[2,2,320,768]{3,2,1,0:T(8,128)} %fusion.23) | copy-start | bytes 11796484
  152.6 13.4 %copy-start.2 = (f32[2,768,768]{2,1,0:T(8,128)S(1)}, f32[2,768,768]{2,1,0:T(8,128)}, u32[]{:S(2)}) copy-start(f32[2,768,768]{2,1,0:T(8,128)} %all-gather.5.cloned.1.call-done) | copy-start | bytes 14155780
  188.7 5.0 copy-start.6
  188.7 85.0 %all-to-all-start = ((f32[3,2,1,768,320]{4,1,0,2,3:T(2,128)}), f32[3,2,1,768,320]{4,1,0,2,3:T(2,128)}, u32[]{:S(2)}, u32[]{:S(2)}) async-start(f32[3,2,1,768,320]{4,1,0,2,3:T(2,128)} %copy.41), calls=%async_computation | async-start | bytes 14155776 | tf_op jit(solution)/shard_map/all_to_all | solution.py:127
  308.3 13.7 %copy-start.1 = (f32[96,30,128]{2,0,1:T(8,128)S(1)}, f32[96,30,128]{2,0,1:T(8,128)}, u32[]{:S(2)}) copy-start(f32[96,30,128]{2,0,1:T(8,128)} %copy.47) | copy-start | bytes 4423684
  329.7 5.4 %copy-start.9 = (f32[30,128]{1,0:T(8,128)S(1)}, f32[30,128]{1,0:T(8,128)}, u32[]{:S(2)}) copy-start(f32[30,128]{1,0:T(8,128)} %fusion.69) | copy-start | bytes 46084
  335.0 1.8 copy-start.7
  335.1 1.8 copy-start.8
  485.0 5.0 copy-start.3
  486.9 3.1 copy-start.4
  486.9 3.1 copy-start.5
Sparse Core Ops, SparseCore 0:
  9.6 53.1 all-gather.2
  64.4 88.2 all-gather.4
where the time goes:
time: 506 us; the launch traced here: 500 us
  waiting for transfers between devices  203 us (40%)
  blocking collectives  94 us (19%)
  local copies, waits for them, and re-layouts  88.7 us (18%)
  matrix products  74.6 us (15%)
  other arithmetic  20.4 us (4%)
  between operations  14.8 us (3%)
    all_to_all x1, blocking collectives, shards(): lax.all_to_all(result, 'row', split_axis=4, concat_axis=3, tiled=True)  94 us
    all_gather x1, waiting for transfers between devices, shards(): block_rows = lax.all_gather(back_maps, 'col', axis=1, tiled=True)  76.1 us
    all_to_all x1, waiting for transfers between devices, shards(): lax.all_to_all(fields, 'row', split_axis=3, concat_axis=4, tiled=True)  71.9 us
    all_gather x1, waiting for transfers between devices, shards(): lax.all_gather(forward_map, 'col', axis=0, tiled=True)  53.2 us
    another operation x2, local copies, waits for them, and re-layouts  16.4 us
    dot_general x1, matrix products, shards(): jnp.einsum('fcxkn,jn->fcxkj', sources, lax.all_gather(forward_map, 'col',...  13.7 us
    dot_general x1, matrix products, spanwise_pass(): jnp.einsum('cnds,fdxyas->fcxyan', fine_fwd, data, precision=lax.Precision...  13.7 us
    dot_general x1, matrix products, shards(): jnp.einsum('yj,fcxkj->fcxyk', block_rows[0], coeffs, precision=lax.Precis...  13.3 us
  transfers between devices with their start and end apart: 3, of which 3 were waited for; matrix products, arithmetic and copies ran while one was open for 5% of the time, Pallas kernels for 0%

commit v1 on v0

--- a/solution.py
+++ b/solution.py
@@ -129,7 +129,10 @@
         (1.0 / (1.0 + penalty)).reshape(local_y, 128, count_z // 128), (0, 2, 1)
     )
     result = spanwise_pass(spanwise, factor_grid, count_z)
-    returned = lax.all_to_all(result, "row", split_axis=4, concat_axis=3, tiled=True)
+    returned = jnp.concatenate(
+        lax.all_to_all(jnp.stack(jnp.split(result, lax.axis_size("row"), axis=4)), "row", 0, 0),
+        axis=3,
+    )
     v_part = returned[1]
     omega_part = form_vorticity(flow_column, span_row, returned[0], returned[2])
     return (jnp.transpose(v_part, (0, 1, 3, 2)), jnp.transpose(omega_part, (0, 1, 3, 2)))

time: 506 us -> 478 us (0.945)
  local copies, waits for them, and re-layouts: 88.7 us -> 74.2 us
  blocking collectives: 94 us -> 82.8 us
    all_to_all x1, blocking collectives: 94 us -> 82.8 us  [shards(): lax.all_to_all(jnp.stack(jnp.split(result, lax.axis_size('row'), axis=4))...]
    all_to_all x1 -> x0, local copies, waits for them, and re-layouts: 9.87 us -> none  [shards(): lax.all_to_all(result, 'row', split_axis=4, concat_axis=3, tiled=True)]
    split x0 -> x1, local copies, waits for them, and re-layouts: none -> 7.24 us  [shards(): jnp.split(result, lax.axis_size('row'), axis=4)]
    another operation x2 -> x3, local copies, waits for them, and re-layouts: 16.4 us -> 16.5 us
where the time goes in v1:
time: 478 us; the launch traced here: 472 us
  waiting for transfers between devices  203 us (42%)
  blocking collectives  82.8 us (17%)
  matrix products  74.6 us (16%)
  local copies, waits for them, and re-layouts  74.2 us (16%)
  other arithmetic  18.3 us (4%)
  between operations  14.9 us (3%)
  starting transfers between devices  5.06 us (1%)
    all_to_all x1, blocking collectives, shards(): lax.all_to_all(jnp.stack(jnp.split(result, lax.axis_size('row'), axis=4))...  82.8 us
    all_gather x1, waiting for transfers between devices, shards(): block_rows = lax.all_gather(back_maps, 'col', axis=1, tiled=True)  76.1 us
    all_to_all x1, waiting for transfers between devices, shards(): lax.all_to_all(fields, 'row', split_axis=3, concat_axis=4, tiled=True)  71.9 us
    all_gather x1, waiting for transfers between devices, shards(): lax.all_gather(forward_map, 'col', axis=0, tiled=True)  53.2 us
    another operation x2, local copies, waits for them, and re-layouts  16.4 us
    dot_general x1, matrix products, shards(): jnp.einsum('fcxkn,jn->fcxkj', sources, lax.all_gather(forward_map, 'col',...  13.7 us
    dot_general x1, matrix products, spanwise_pass(): jnp.einsum('cnds,fdxyas->fcxyan', fine_fwd, data, precision=lax.Precision...  13.7 us
    dot_general x1, matrix products, shards(): jnp.einsum('yj,fcxkj->fcxyk', block_rows[0], coeffs, precision=lax.Precis...  13.3 us
  transfers between devices with their start and end apart: 3, of which 3 were waited for; matrix products, arithmetic and copies ran while one was open for 5% of the time, Pallas kernels for 0%

profile of v1, /device:TPU:0, one launch (start us, length us, event | category | flops | bytes accessed | tf_op | source)
XLA Modules:
  0.0 472.4 jit_solution(1457501060607295183)
XLA Ops:
  7.2 0.0 all-gather.3.cloned.1.call-start
  7.2 0.7 all-gather.3.cloned.1.call-update
  7.9 0.0 all-gather.5.cloned.1.call-start
  7.9 0.7 all-gather.5.cloned.1.call-update
  8.7 0.7 broadcast_add_fusion
  9.4 0.2 add_divide_fusion.2
  9.6 53.2 %all-gather.3.cloned.1.call-done = f32[768,768]{1,0:T(8,128)} async-done(((f32[192,768]{1,0:T(8,128)}), f32[768,768]{1,0:T(8,128)}) %all-gather.3.cloned.1.call-update) | async-done | bytes 2359312 | tf_op jit(solution)/shard_map/all_gather | solution.py:116
  62.8 13.7 %fusion.23 = f32[2,2,320,768]{3,2,1,0:T(8,128)} fusion(f32[768,768]{1,0:T(8,128)} %all-gather.3.cloned.1.call-done, f32[1,2,1,320,768]{4,3,1,0,2:T(8,128)} %bitcast.224, f32[1,2,1,320,768]{4,3,1,0,2:T(8,128)} %bitcast.225, f32[320,768]{1,0:T(8,128)S(1)} %add_divide_fusion.2), kind=kOutput, calls=%fused_computation.31 | convolution fusion | flops 9061662720 | bytes 11206656 | tf_op jit(solution)/shard_map/fcxkn,jn->fcxkj/dot_general | solution.py:113
  76.5 76.1 %all-gather.5.cloned.1.call-done = f32[2,768,768]{2,1,0:T(8,128)} async-done(((f32[2,192,768]{2,1,0:T(8,128)}), f32[2,768,768]{2,1,0:T(8,128)}) %all-gather.5.cloned.1.call-update) | async-done | bytes 4718608 | tf_op jit(solution)/shard_map/all_gather | solution.py:120
  152.6 13.3 %fusion.21 = f32[2,2,320,768]{3,2,1,0:T(8,128)S(1)} fusion(f32[2,2,320,768]{3,2,1,0:T(8,128)} %fusion.23, f32[2,768,768]{2,1,0:T(8,128)} %all-gather.5.cloned.1.call-done), kind=kOutput, calls=%fused_computation.29 | convolution fusion | flops 9059696640 | bytes 10223616 | tf_op jit(solution)/shard_map/yj,fcxkj->fcxyk/dot_general | solution.py:121
  165.9 0.1 slice.98
  166.0 5.5 %fusion.26 = f32[2,1,768,320]{2,3,0,1:T(8,128)S(1)} fusion(f32[2,768,768]{2,1,0:T(8,128)S(1)} %copy-done.2, f32[2,2,320,768]{3,2,1,0:T(8,128)S(1)} %copy-done), kind=kOutput, calls=%fused_computation.36 | convolution fusion | flops 4529848320 | bytes 6291456 | tf_op jit(solution)/shard_map/yj,cxkj->cxyk/dot_general | solution.py:122
  171.5 0.7 subtract_divide_fusion.1
  172.2 0.1 maximum_bitcast_fusion.9
  172.4 0.1 maximum_bitcast_fusion.10
  172.5 3.0 pad_maximum_fusion
  175.5 13.2 %copy.45 = f32[3,2,1,768,320]{4,1,0,2,3:T(2,128)} copy(f32[3,2,1,768,320]{3,4,1,0,2:T(8,128)} %pad_maximum_fusion) | data formatting | bytes 11796480 | tf_op jit(solution)/shard_map/stack | solution.py:126
  188.7 5.0 %all-to-all-start = ((f32[3,2,1,768,320]{4,1,0,2,3:T(2,128)}), f32[3,2,1,768,320]{4,1,0,2,3:T(2,128)}, u32[]{:S(2)}, u32[]{:S(2)}) async-start(f32[3,2,1,768,320]{4,1,0,2,3:T(2,128)} %copy.45), calls=%async_computation | async-start | bytes 14155776 | tf_op jit(solution)/shard_map/all_to_all | solution.py:127
  193.7 0.0 copy-done.6
  193.7 0.2 add_divide_fusion
  193.9 1.8 copy.50
  195.6 1.6 reshape.761
  197.2 1.8 copy.51
  199.0 0.7 fusion.77
  199.7 0.7 fusion.67
  200.4 0.3 fusion.57
  200.7 0.1 fusion.78
  200.8 0.6 fusion.61
  201.4 0.3 fusion.55
  201.8 71.9 %all-to-all-done = f32[3,2,1,768,320]{4,1,0,2,3:T(2,128)} async-done(((f32[3,2,1,768,320]{4,1,0,2,3:T(2,128)}), f32[3,2,1,768,320]{4,1,0,2,3:T(2,128)}, u32[]{:S(2)}, u32[]{:S(2)}) %all-to-all-start) | async-done | bytes 5898272 | tf_op jit(solution)/shard_map/all_to_all | solution.py:127
  273.7 3.5 copy.46
  277.2 7.0 %copy.75 = f32[3,2,1,96,8,320]{5,4,1,3,0,2:T(8,128)} copy(f32[3,2,1,96,8,320]{5,3,4,1,0,2:T(8,128)S(1)} %bitcast.215) | data formatting | bytes 11796480 | tf_op jit(solution)/shard_map/reshape.29
  284.1 9.5 %reshape.769 = f32[3,2,96,20,128,1]{4,3,1,2,0,5:T(8,128)} reshape(f32[3,2,1,96,8,320]{5,4,1,3,0,2:T(8,128)} %copy.75) | data formatting | bytes 11796480 | tf_op jit(solution)/shard_map/reshape.29
  293.6 10.7 %fusion.13 = f32[3,2,1,96,30,128]{5,4,1,3,0,2:T(8,128)S(1)} fusion(f32[3,2,96,20,128,1]{4,3,1,2,0,5:T(8,128)} %reshape.769, f32[1,30,2,20]{1,3,2,0:T(8,128)S(1)} %get-tuple-element.35, f32[1,30,2,20]{1,3,2,0:T(8,128)S(1)} %get-tuple-element.38), kind=kOutput, calls=%fused_computation.23 | convolution fusion | flops 1061685632 | bytes 14755200 | tf_op jit(solution)/shard_map/cadk,fdxyks->fcxyas/dot_general | solution.py:82
  304.3 2.5 multiply_subtract_fusion.1
  306.8 1.6 maximum_bitcast_fusion
  308.3 0.0 copy-start.1
  308.3 13.7 %fusion.5 = f32[3,96,30,2,128,1]{4,1,5,3,2,0:T(8,128)S(1)} fusion(f32[3,2,96,30,128,1]{4,3,1,2,0,5:T(8,128)S(1)} %maximum_bitcast_fusion, f32[1,128,2,128]{3,1,2,0:T(8,128)S(1)} %get-tuple-element.29, f32[1,128,2,128]{3,1,2,0:T(8,128)S(1)} %get-tuple-element.32), kind=kOutput, calls=%fused_computation.9 | convolution fusion | flops 6794838016 | bytes 17956864 | tf_op jit(solution)/shard_map/cnds,fdxyas->fcxyan/dot_general | solution.py:84
  322.1 7.6 %fusion.16 = f32[3,96,30,2,128]{4,1,3,2,0:T(8,128)S(1)} fusion(f32[3,96,30,2,128,1]{4,1,5,3,2,0:T(8,128)S(1)} %fusion.5, f32[96,30,128]{2,0,1:T(8,128)S(1)} %copy-done.1, f32[1,128,2,128]{3,1,2,0:T(8,128)S(1)} %get-tuple-element.33, f32[1,128,2,128]{3,1,2,0:T(8,128)S(1)} %get-tuple-element.28), kind=kOutput, calls=%fused_computation.24 | convolution fusion | flops 6797049856 | bytes 19431424 | tf_op jit(solution)/shard_map/ckdn,fdxyan->fcxyak/dot_general | solution.py:86
  329.7 5.4 %copy.115 = f32[3,96,30,2,128]{4,2,3,1,0:T(8,128)S(1)} copy(f32[3,96,30,2,128]{4,1,3,2,0:T(8,128)S(1)} %fusion.16) | data formatting | bytes 17694720 | tf_op jit(solution)/shard_map/ckdn,fdxyan->fcxyak/dot_general | solution.py:86
  335.1 0.0 copy-start.7
  335.1 1.8 multiply_subtract_fusion
  336.9 10.1 %fusion.19 = f32[3,2,1,96,20,128]{5,4,1,3,0,2:T(8,128)} fusion(f32[3,1,1,96,30,128]{5,4,1,3,0,2:T(8,128)S(1)} %get-tuple-element.9, f32[3,1,1,96,30,128]{5,4,1,3,0,2:T(8,128)S(1)} %get-tuple-element.8, f32[1,30,2,20]{1,3,2,0:T(8,128)S(1)} %copy-done.8, f32[1,30,2,20]{1,3,2,0:T(8,128)S(1)} %copy-done.7), kind=kOutput, calls=%fused_computation.25 | convolution fusion | flops 1063899840 | bytes 14755200 | tf_op jit(solution)/shard_map/cdak,fdxyas->fcxyks/dot_general | solution.py:88
  347.0 8.7 %reshape.783 = f32[3,2,1,96,2560]{4,1,3,0,2:T(2,128)} reshape(f32[3,2,1,96,20,128]{5,4,1,3,0,2:T(8,128)} %fusion.19) | data formatting | bytes 11796480 | tf_op jit(solution)/shard_map/reshape | solution.py:89
  355.7 7.2 %fusion.90 = (f32[3,2,1,96,320]{4,1,3,0,2:T(2,128)S(1)}, f32[3,2,1,96,320]{4,1,3,0,2:T(2,128)S(1)}, f32[3,2,1,96,320]{4,1,3,0,2:T(2,128)S(1)}, f32[3,2,1,96,320]...) fusion(f32[3,2,1,96,2560]{4,1,3,0,2:T(2,128)} %reshape.783), kind=kLoop, calls=%fused_computation.142 | loop fusion | bytes 11796480 | tf_op jit(solution)/shard_map/split | solution.py:133
  363.0 0.1 fusion.34
  363.0 0.1 fusion.33
  363.1 0.1 fusion.32
  363.2 0.1 fusion.31
  363.2 0.1 fusion.30
  363.3 0.1 fusion.29
  363.4 0.1 fusion.28
  363.4 0.1 fusion.27
  363.5 82.8 %all_to_all.20 = f32[8,3,2,1,96,320]{5,4,2,1,3,0:T(8,128)S(1)} all-to-all(f32[8,3,2,1,96,320]{5,4,2,1,3,0:T(8,128)S(1)} %fusion.27), channel_id=1, replica_groups=mesh['row'=8,'col'=4] {'row'}, dimensions={0} | all-to-all | bytes 11796480 | tf_op jit(solution)/shard_map/all_to_all | solution.py:133
  446.3 1.9 fusion.89
  448.2 0.2 slice.103
  448.5 2.6 copy.55
  451.0 2.6 copy.56
  453.6 2.6 copy.57
  456.2 1.3 copy.58
  457.5 1.6 copy.54
  459.1 3.1 copy.59
  462.2 1.5 multiply_subtract_fusion.3
  463.7 1.4 maximum_bitcast_fusion.11
  (21 shorter events, 0.1 us)
Async XLA Ops:
  7.2 55.6 %all-gather.3.cloned.1.call-start = ((), (), s32[]{:S(2)}) async-start(), calls=%async_computation.2 | async-start | bytes 2949120 | tf_op jit(solution)/shard_map/all_gather | solution.py:116
  7.9 144.7 %all-gather.5.cloned.1.call-start = ((), (), s32[]{:S(2)}) async-start(), calls=%async_computation.3 | async-start | bytes 5898240 | tf_op jit(solution)/shard_map/all_gather | solution.py:120
  152.6 13.4 %copy-start = (f32[2,2,320,768]{3,2,1,0:T(8,128)S(1)}, f32[2,2,320,768]{3,2,1,0:T(8,128)}, u32[]{:S(2)}) copy-start(f32[2,2,320,768]{3,2,1,0:T(8,128)} %fusion.23) | copy-start | bytes 11796484
  152.6 13.4 %copy-start.2 = (f32[2,768,768]{2,1,0:T(8,128)S(1)}, f32[2,768,768]{2,1,0:T(8,128)}, u32[]{:S(2)}) copy-start(f32[2,768,768]{2,1,0:T(8,128)} %all-gather.5.cloned.1.call-done) | copy-start | bytes 14155780
  188.7 5.0 %copy-start.6 = (f32[96,3840]{1,0:T(8,128)S(1)}, f32[96,3840]{1,0:T(8,128)}, u32[]{:S(2)}) copy-start(f32[96,3840]{1,0:T(8,128)} %param.11) | copy-start | bytes 4423684
  188.7 85.0 %all-to-all-start = ((f32[3,2,1,768,320]{4,1,0,2,3:T(2,128)}), f32[3,2,1,768,320]{4,1,0,2,3:T(2,128)}, u32[]{:S(2)}, u32[]{:S(2)}) async-start(f32[3,2,1,768,320]{4,1,0,2,3:T(2,128)} %copy.45), calls=%async_computation | async-start | bytes 14155776 | tf_op jit(solution)/shard_map/all_to_all | solution.py:127
  308.3 13.7 %copy-start.1 = (f32[96,30,128]{2,0,1:T(8,128)S(1)}, f32[96,30,128]{2,0,1:T(8,128)}, u32[]{:S(2)}) copy-start(f32[96,30,128]{2,0,1:T(8,128)} %copy.51) | copy-start | bytes 4423684
  329.7 5.4 %copy-start.9 = (f32[30,128]{1,0:T(8,128)S(1)}, f32[30,128]{1,0:T(8,128)}, u32[]{:S(2)}) copy-start(f32[30,128]{1,0:T(8,128)} %fusion.77) | copy-start | bytes 46084
  335.1 1.8 copy-start.7
  335.1 1.8 copy-start.8
  457.5 4.7 copy-start.3
  459.1 3.1 copy-start.4
  459.1 3.1 copy-start.5
Sparse Core Ops, SparseCore 0:
  9.6 53.1 all-gather.2
  64.4 88.2 all-gather.4
